TPU v7x, 512 devices: a whole 4x8x8 slice. The times are simulated.
512 devices in a mesh: band: 8 (over y_lo, core), grid: 64 (over y_hi, x, z).
Axes of the slice: x: 4, y: 8 (y_hi: 2, y_lo: 4; y = y_hi * 4 + y_lo), z: 8, core: 2. Of those that a mesh axis runs over, the one named last changes fastest.
Arguments:
- orbitals: float32 [8, 2, 192, 192, 192], P('band', None, 'grid'), may hold values from -6 to 6
- occupations: float32 [8], P('band'), may hold values from 0.5 to 2
- ion_potential: float32 [192, 192, 192], P('grid'), may hold values from -0.6 to 0.6
- hxc_potential: float32 [192, 192, 192], P('grid'), may hold values from -0.4 to 0.4
Outputs:
- new_orbitals: float32 [8, 2, 192, 192, 192], P('band', None, 'grid')
- new_potential: float32 [192, 192, 192], P('grid')
All inputs are finite; a program needn't handle non-finite values.
Results may differ from a plain program's by a relative error of at most 0.0003.
Values sent between devices are 32-bit elements; how exact they have to be, the bound alone decides.
A program may use at most 64 MiB of HBM per device.

v0:
```python
import math
import jax
import jax.numpy as jnp
from jax import lax
from jax.sharding import PartitionSpec as P

BESSEL_ZERO = 0.8462873527504802
BESSEL_ONE = 0.36884204609417703
BESSEL_TWO = 0.07581776248
XC_FACTOR = 0.98474502


def tables(length):
    idx = jnp.arange(length, dtype=jnp.int32)
    angle = (idx[:, None] * idx[None, :] % length).astype(jnp.float32) * (2.0 * math.pi / length)
    return (jnp.cos(angle), jnp.sin(angle))


def transform(real_part, imag_part, form, inverse, length):
    cosine, sine = tables(length)
    high = lax.Precision.HIGHEST
    rc = jnp.einsum(form, real_part, cosine, precision=high)
    rs = jnp.einsum(form, real_part, sine, precision=high)
    ic = jnp.einsum(form, imag_part, cosine, precision=high)
    isn = jnp.einsum(form, imag_part, sine, precision=high)
    if inverse:
        scale = 1.0 / length
        return ((rc - isn) * scale, (ic + rs) * scale)
    return (rc + isn, ic - rs)


def along_z(real_part, imag_part, inverse):
    return transform(real_part, imag_part, "oxyn,nk->oxyk", inverse, real_part.shape[3])


def along_y(real_part, imag_part, inverse):
    return transform(real_part, imag_part, "oxnz,nk->oxkz", inverse, real_part.shape[2])


def along_x(real_part, imag_part, inverse):
    return transform(real_part, imag_part, "onyz,nk->okyz", inverse, real_part.shape[1])


def forward(real_part, imag_part):
    real_part, imag_part = along_z(real_part, imag_part, False)
    real_part, imag_part = along_y(real_part, imag_part, False)
    real_part, imag_part = (
        lax.all_to_all(real_part, "grid", split_axis=2, concat_axis=1, tiled=True),
        lax.all_to_all(imag_part, "grid", split_axis=2, concat_axis=1, tiled=True),
    )
    return along_x(real_part, imag_part, False)


def backward(real_part, imag_part):
    real_part, imag_part = along_x(real_part, imag_part, True)
    real_part, imag_part = (
        lax.all_to_all(real_part, "grid", split_axis=1, concat_axis=2, tiled=True),
        lax.all_to_all(imag_part, "grid", split_axis=1, concat_axis=2, tiled=True),
    )
    real_part, imag_part = along_y(real_part, imag_part, True)
    real_part, imag_part = along_z(real_part, imag_part, True)
    return (real_part, imag_part)


def frequency(idx, length):
    return jnp.where(idx < length // 2, idx, idx - length).astype(jnp.float32)


def squares_block(x_count, y_start, y_count, length):
    fx = frequency(jnp.arange(x_count, dtype=jnp.int32), length)
    fy = frequency(y_start + jnp.arange(y_count, dtype=jnp.int32), length)
    fz = frequency(jnp.arange(length, dtype=jnp.int32), length)
    return (fx * fx)[:, None, None] + (fy * fy)[None, :, None] + (fz * fz)[None, None, :]


def hartree_filter(squares, length):
    return jnp.where(squares > 0, length * math.sqrt(length) / 16.0 / (squares + 1.0), 0.0)


def local(orbitals, occupations, ion_potential, hxc_potential):
    length = orbitals.shape[-1]
    columns = length // lax.axis_size("grid")
    grid_pos = lax.axis_index("grid")
    squares = squares_block(length, grid_pos * columns, columns, length)
    kinetic = 2.0 * squares / (3.0 * (length / 2) ** 2) - 1.0
    potential = ion_potential + hxc_potential

    def hamilton(real_part, imag_part):
        fre, fim = forward(real_part, imag_part)
        back_re, back_im = backward(kinetic * fre, kinetic * fim)
        return (back_re + potential * real_part, back_im + potential * imag_part)

    psi_re = orbitals[:, 0]
    psi_im = orbitals[:, 1]
    first_re, first_im = hamilton(psi_re, psi_im)
    again_re, again_im = hamilton(first_re, first_im)
    second_re = 2.0 * again_re - psi_re
    second_im = 2.0 * again_im - psi_im
    fresh_re = BESSEL_ZERO * psi_re + 2.0 * BESSEL_ONE * first_im - 2.0 * BESSEL_TWO * second_re
    fresh_im = BESSEL_ZERO * psi_im - 2.0 * BESSEL_ONE * first_re - 2.0 * BESSEL_TWO * second_im
    new_orbitals = jnp.stack([fresh_re, fresh_im], axis=1)
    partial_value = jnp.sum(
        occupations[:, None, None, None] * (fresh_re * fresh_re + fresh_im * fresh_im), axis=0
    )
    density = lax.psum(partial_value, "band")
    fre, fim = forward(density[None], jnp.zeros_like(density)[None])
    kernel = hartree_filter(squares, length)
    hart_re, hart_im = backward(kernel * fre, kernel * fim)
    new_potential = hart_re[0] - XC_FACTOR * jnp.cbrt(density)
    return (new_orbitals, new_potential)


def solution(mesh):
    placed = (
        P("band", None, "grid", None, None),
        P("band"),
        P("grid", None, None),
        P("grid", None, None),
    )
    return jax.shard_map(
        local,
        mesh=mesh,
        in_specs=placed,
        out_specs=(P("band", None, "grid", None, None), P("grid", None, None)),
        check_vma=False,
    )
```

profile of v0, /device:TPU:6, one launch (start us, length us, event | category | flops | bytes accessed | tf_op | source)
XLA Modules:
  0.0 574.2 jit_solution(15256407723588242375)
XLA Ops:
  7.2 3.1 fusion.63
  10.3 2.0 fusion.60
  12.3 2.0 fusion.54
  14.3 2.0 fusion.55
  16.3 2.0 fusion.170
  18.2 2.0 fusion.53
  20.2 1.9 copy.242
  22.1 19.1 %all-to-all-start = ((f32[1,3,192,192]{3,0,1,2:T(1,128)}), f32[1,3,192,192]{3,0,1,2:T(1,128)S(1)}, u32[]{:S(2)}, u32[]{:S(2)}) async-start(f32[1,3,192,192]{3,0,1,2:T(1,128)} %copy.242), calls=%async_computation | async-start | bytes 1179648 | tf_op jit(solution)/shard_map/all_to_all | solution.py:49
  41.2 2.0 fusion.166
  43.2 2.0 fusion.52
  46.6 14.3 %all-to-all-done = f32[1,3,192,192]{3,0,1,2:T(1,128)S(1)} async-done(((f32[1,3,192,192]{3,0,1,2:T(1,128)}), f32[1,3,192,192]{3,0,1,2:T(1,128)S(1)}, u32[]{:S(2)}, u32[]{:S(2)}) %all-to-all-start) | async-done | bytes 442400 | tf_op jit(solution)/shard_map/all_to_all | solution.py:49
  60.9 9.6 %all-to-all-start.1 = ((f32[1,3,192,192]{3,0,1,2:T(1,128)}), f32[1,3,192,192]{3,0,1,2:T(1,128)S(1)}, u32[]{:S(2)}, u32[]{:S(2)}) async-start(f32[1,3,192,192]{3,0,1,2:T(1,128)} %copy.250), calls=%async_computation.1 | async-start | bytes 1179648 | tf_op jit(solution)/shard_map/all_to_all | solution.py:48
  71.8 19.9 %all-to-all-done.1 = f32[1,3,192,192]{3,0,1,2:T(1,128)S(1)} async-done(((f32[1,3,192,192]{3,0,1,2:T(1,128)}), f32[1,3,192,192]{3,0,1,2:T(1,128)S(1)}, u32[]{:S(2)}, u32[]{:S(2)}) %all-to-all-start.1) | async-done | bytes 442400 | tf_op jit(solution)/shard_map/all_to_all | solution.py:48
  104.9 8.0 %all-to-all-start.3 = ((f32[1,192,3,192]{3,0,2,1:T(1,128)}), f32[1,192,3,192]{3,0,2,1:T(1,128)S(1)}, u32[]{:S(2)}, u32[]{:S(2)}) async-start(f32[1,192,3,192]{3,0,2,1:T(1,128)} %copy.263), calls=%async_computation.3 | async-start | bytes 1179648 | tf_op jit(solution)/shard_map/all_to_all | solution.py:57
  117.3 16.8 %all-to-all-done.3 = f32[1,192,3,192]{3,0,2,1:T(1,128)S(1)} async-done(((f32[1,192,3,192]{3,0,2,1:T(1,128)}), f32[1,192,3,192]{3,0,2,1:T(1,128)S(1)}, u32[]{:S(2)}, u32[]{:S(2)}) %all-to-all-start.3) | async-done | bytes 442400 | tf_op jit(solution)/shard_map/all_to_all | solution.py:57
  134.1 7.9 %all-to-all-start.2 = ((f32[1,192,3,192]{3,0,2,1:T(1,128)}), f32[1,192,3,192]{3,0,2,1:T(1,128)}, u32[]{:S(2)}, u32[]{:S(2)}) async-start(f32[1,192,3,192]{3,0,2,1:T(1,128)} %copy.258), calls=%async_computation.2 | async-start | bytes 1179648 | tf_op jit(solution)/shard_map/all_to_all | solution.py:58
  143.7 19.3 %all-to-all-done.2 = f32[1,192,3,192]{3,0,2,1:T(1,128)} async-done(((f32[1,192,3,192]{3,0,2,1:T(1,128)}), f32[1,192,3,192]{3,0,2,1:T(1,128)}, u32[]{:S(2)}, u32[]{:S(2)}) %all-to-all-start.2) | async-done | bytes 442400 | tf_op jit(solution)/shard_map/all_to_all | solution.py:58
  163.1 2.1 copy.259
  176.6 1.6 fusion.41
  188.9 8.1 %all-to-all-start.4 = ((f32[1,3,192,192]{3,0,1,2:T(1,128)}), f32[1,3,192,192]{3,0,1,2:T(1,128)}, u32[]{:S(2)}, u32[]{:S(2)}) async-start(f32[1,3,192,192]{3,0,1,2:T(1,128)} %copy.270), calls=%async_computation.4 | async-start | bytes 1179648 | tf_op jit(solution)/shard_map/all_to_all | solution.py:48
  201.3 16.4 %all-to-all-done.4 = f32[1,3,192,192]{3,0,1,2:T(1,128)} async-done(((f32[1,3,192,192]{3,0,1,2:T(1,128)}), f32[1,3,192,192]{3,0,1,2:T(1,128)}, u32[]{:S(2)}, u32[]{:S(2)}) %all-to-all-start.4) | async-done | bytes 442400 | tf_op jit(solution)/shard_map/all_to_all | solution.py:48
  217.8 8.3 %all-to-all-start.5 = ((f32[1,3,192,192]{3,0,1,2:T(1,128)}), f32[1,3,192,192]{3,0,1,2:T(1,128)}, u32[]{:S(2)}, u32[]{:S(2)}) async-start(f32[1,3,192,192]{3,0,1,2:T(1,128)} %copy.276), calls=%async_computation.5 | async-start | bytes 1179648 | tf_op jit(solution)/shard_map/all_to_all | solution.py:49
  230.3 16.8 %all-to-all-done.5 = f32[1,3,192,192]{3,0,1,2:T(1,128)} async-done(((f32[1,3,192,192]{3,0,1,2:T(1,128)}), f32[1,3,192,192]{3,0,1,2:T(1,128)}, u32[]{:S(2)}, u32[]{:S(2)}) %all-to-all-start.5) | async-done | bytes 442400 | tf_op jit(solution)/shard_map/all_to_all | solution.py:49
  249.8 2.2 reshape.437
  252.1 2.5 fusion.131
  256.0 2.6 fusion.34
  264.4 8.0 %all-to-all-start.7 = ((f32[1,192,3,192]{3,0,2,1:T(1,128)}), f32[1,192,3,192]{3,0,2,1:T(1,128)}, u32[]{:S(2)}, u32[]{:S(2)}) async-start(f32[1,192,3,192]{3,0,2,1:T(1,128)} %copy.289), calls=%async_computation.7 | async-start | bytes 1179648 | tf_op jit(solution)/shard_map/all_to_all | solution.py:58
  272.4 2.5 fusion.139
  277.8 15.7 %all-to-all-done.7 = f32[1,192,3,192]{3,0,2,1:T(1,128)} async-done(((f32[1,192,3,192]{3,0,2,1:T(1,128)}), f32[1,192,3,192]{3,0,2,1:T(1,128)}, u32[]{:S(2)}, u32[]{:S(2)}) %all-to-all-start.7) | async-done | bytes 442400 | tf_op jit(solution)/shard_map/all_to_all | solution.py:58
  293.5 7.9 %all-to-all-start.6 = ((f32[1,192,3,192]{3,0,2,1:T(1,128)}), f32[1,192,3,192]{3,0,2,1:T(1,128)}, u32[]{:S(2)}, u32[]{:S(2)}) async-start(f32[1,192,3,192]{3,0,2,1:T(1,128)} %copy.284), calls=%async_computation.6 | async-start | bytes 1179648 | tf_op jit(solution)/shard_map/all_to_all | solution.py:57
  302.2 2.1 copy.290
  305.7 16.7 %all-to-all-done.6 = f32[1,192,3,192]{3,0,2,1:T(1,128)} async-done(((f32[1,192,3,192]{3,0,2,1:T(1,128)}), f32[1,192,3,192]{3,0,2,1:T(1,128)}, u32[]{:S(2)}, u32[]{:S(2)}) %all-to-all-start.6) | async-done | bytes 442400 | tf_op jit(solution)/shard_map/all_to_all | solution.py:57
  322.5 2.1 copy.285
  324.6 2.2 reshape.438
  326.9 2.5 fusion.141
  336.5 1.5 fusion.25
  338.0 3.0 add_multiply_fusion.1
  342.5 69.9 %all-reduce.2.cloned.1.call-done = f32[3,192,192]{2,1,0:T(8,128)} async-done(((f32[3,192,192]{2,1,0:T(8,128)}), f32[3,192,192]{2,1,0:T(8,128)}) %all-reduce.2.cloned.1.call-update) | async-done | bytes 442384 | tf_op jit(solution)/shard_map/psum | solution.py:105
  412.4 2.5 fusion.148
  422.1 14.0 %all-to-all-start.9 = ((f32[1,3,192,192]{3,0,1,2:T(1,128)}), f32[1,3,192,192]{3,0,1,2:T(1,128)}, u32[]{:S(2)}, u32[]{:S(2)}) async-start(f32[1,3,192,192]{3,0,1,2:T(1,128)} %copy.302), calls=%async_computation.9 | async-start | bytes 1179648 | tf_op jit(solution)/shard_map/all_to_all | solution.py:49
  440.3 16.0 %all-to-all-done.9 = f32[1,3,192,192]{3,0,1,2:T(1,128)} async-done(((f32[1,3,192,192]{3,0,1,2:T(1,128)}), f32[1,3,192,192]{3,0,1,2:T(1,128)}, u32[]{:S(2)}, u32[]{:S(2)}) %all-to-all-start.9) | async-done | bytes 442400 | tf_op jit(solution)/shard_map/all_to_all | solution.py:49
  456.3 7.8 %all-to-all-start.8 = ((f32[1,3,192,192]{3,0,1,2:T(1,128)}), f32[1,3,192,192]{3,0,1,2:T(1,128)S(1)}, u32[]{:S(2)}, u32[]{:S(2)}) async-start(f32[1,3,192,192]{3,0,1,2:T(1,128)} %copy.296), calls=%async_computation.8 | async-start | bytes 1179648 | tf_op jit(solution)/shard_map/all_to_all | solution.py:48
  466.4 19.1 %all-to-all-done.8 = f32[1,3,192,192]{3,0,1,2:T(1,128)S(1)} async-done(((f32[1,3,192,192]{3,0,1,2:T(1,128)}), f32[1,3,192,192]{3,0,1,2:T(1,128)S(1)}, u32[]{:S(2)}, u32[]{:S(2)}) %all-to-all-start.8) | async-done | bytes 442400 | tf_op jit(solution)/shard_map/all_to_all | solution.py:48
  496.8 7.8 %all-to-all-start.10 = ((f32[1,192,3,192]{3,0,2,1:T(1,128)}), f32[1,192,3,192]{3,0,2,1:T(1,128)}, u32[]{:S(2)}, u32[]{:S(2)}) async-start(f32[1,192,3,192]{3,0,2,1:T(1,128)} %copy.310), calls=%async_computation.10 | async-start | bytes 1179648 | tf_op jit(solution)/shard_map/all_to_all | solution.py:57
  509.0 16.9 %all-to-all-done.10 = f32[1,192,3,192]{3,0,2,1:T(1,128)} async-done(((f32[1,192,3,192]{3,0,2,1:T(1,128)}), f32[1,192,3,192]{3,0,2,1:T(1,128)}, u32[]{:S(2)}, u32[]{:S(2)}) %all-to-all-start.10) | async-done | bytes 442400 | tf_op jit(solution)/shard_map/all_to_all | solution.py:57
  526.0 7.6 %all-to-all-start.11 = ((f32[1,192,3,192]{3,0,2,1:T(1,128)}), f32[1,192,3,192]{3,0,2,1:T(1,128)S(1)}, u32[]{:S(2)}, u32[]{:S(2)}) async-start(f32[1,192,3,192]{3,0,2,1:T(1,128)} %copy.315), calls=%async_computation.11 | async-start | bytes 1179648 | tf_op jit(solution)/shard_map/all_to_all | solution.py:58
  536.2 18.6 %all-to-all-done.11 = f32[1,192,3,192]{3,0,2,1:T(1,128)S(1)} async-done(((f32[1,192,3,192]{3,0,2,1:T(1,128)}), f32[1,192,3,192]{3,0,2,1:T(1,128)S(1)}, u32[]{:S(2)}, u32[]{:S(2)}) %all-to-all-start.11) | async-done | bytes 442400 | tf_op jit(solution)/shard_map/all_to_all | solution.py:58
  564.4 2.6 fusion.1
  (126 shorter events, 116.3 us)
Async XLA Ops:
  7.2 3.1 copy-start
  22.1 38.8 %all-to-all-start = ((f32[1,3,192,192]{3,0,1,2:T(1,128)}), f32[1,3,192,192]{3,0,1,2:T(1,128)S(1)}, u32[]{:S(2)}, u32[]{:S(2)}) async-start(f32[1,3,192,192]{3,0,1,2:T(1,128)} %copy.242), calls=%async_computation | async-start | bytes 1179648 | tf_op jit(solution)/shard_map/all_to_all | solution.py:49
  60.9 30.8 %all-to-all-start.1 = ((f32[1,3,192,192]{3,0,1,2:T(1,128)}), f32[1,3,192,192]{3,0,1,2:T(1,128)S(1)}, u32[]{:S(2)}, u32[]{:S(2)}) async-start(f32[1,3,192,192]{3,0,1,2:T(1,128)} %copy.250), calls=%async_computation.1 | async-start | bytes 1179648 | tf_op jit(solution)/shard_map/all_to_all | solution.py:48
  104.9 29.2 %all-to-all-start.3 = ((f32[1,192,3,192]{3,0,2,1:T(1,128)}), f32[1,192,3,192]{3,0,2,1:T(1,128)S(1)}, u32[]{:S(2)}, u32[]{:S(2)}) async-start(f32[1,192,3,192]{3,0,2,1:T(1,128)} %copy.263), calls=%async_computation.3 | async-start | bytes 1179648 | tf_op jit(solution)/shard_map/all_to_all | solution.py:57
  115.9 26.2 %copy-start.13 = (f32[3,192,192]{2,1,0:T(8,128)S(1)}, f32[3,192,192]{2,1,0:T(8,128)}, u32[]{:S(2)}) copy-start(f32[3,192,192]{2,1,0:T(8,128)} %param.6) | copy-start | bytes 1327108
  115.9 26.2 %copy-start.14 = (f32[3,192,192]{2,1,0:T(8,128)S(1)}, f32[3,192,192]{2,1,0:T(8,128)}, u32[]{:S(2)}) copy-start(f32[3,192,192]{2,1,0:T(8,128)} %param.7) | copy-start | bytes 1327108
  134.1 8.0 %copy-start.8 = (f32[1,192,3,192]{3,0,2,1:T(1,128)}, f32[1,192,3,192]{3,0,2,1:T(1,128)S(1)}, u32[]{:S(2)}) copy-start(f32[1,192,3,192]{3,0,2,1:T(1,128)S(1)} %all-to-all-done.3) | copy-start | bytes 1327108
  134.1 29.0 %all-to-all-start.2 = ((f32[1,192,3,192]{3,0,2,1:T(1,128)}), f32[1,192,3,192]{3,0,2,1:T(1,128)}, u32[]{:S(2)}, u32[]{:S(2)}) async-start(f32[1,192,3,192]{3,0,2,1:T(1,128)} %copy.258), calls=%async_computation.2 | async-start | bytes 1179648 | tf_op jit(solution)/shard_map/all_to_all | solution.py:58
  183.8 0.8 copy-start.1
  188.9 28.9 %all-to-all-start.4 = ((f32[1,3,192,192]{3,0,1,2:T(1,128)}), f32[1,3,192,192]{3,0,1,2:T(1,128)}, u32[]{:S(2)}, u32[]{:S(2)}) async-start(f32[1,3,192,192]{3,0,1,2:T(1,128)} %copy.270), calls=%async_computation.4 | async-start | bytes 1179648 | tf_op jit(solution)/shard_map/all_to_all | solution.py:48
  197.0 1.4 copy-start.2
  217.8 29.3 %all-to-all-start.5 = ((f32[1,3,192,192]{3,0,1,2:T(1,128)}), f32[1,3,192,192]{3,0,1,2:T(1,128)}, u32[]{:S(2)}, u32[]{:S(2)}) async-start(f32[1,3,192,192]{3,0,1,2:T(1,128)} %copy.276), calls=%async_computation.5 | async-start | bytes 1179648 | tf_op jit(solution)/shard_map/all_to_all | solution.py:49
  230.3 24.3 %copy-start.5 = (f32[192,3,192]{2,0,1:T(8,128)}, f32[192,3,192]{2,0,1:T(8,128)S(1)}, u32[]{:S(2)}) copy-start(f32[192,3,192]{2,0,1:T(8,128)S(1)} %reshape.436) | copy-start | bytes 1327108
  256.0 2.6 copy-start.6
  260.1 1.4 copy-start.3
  264.4 29.1 %all-to-all-start.7 = ((f32[1,192,3,192]{3,0,2,1:T(1,128)}), f32[1,192,3,192]{3,0,2,1:T(1,128)}, u32[]{:S(2)}, u32[]{:S(2)}) async-start(f32[1,192,3,192]{3,0,2,1:T(1,128)} %copy.289), calls=%async_computation.7 | async-start | bytes 1179648 | tf_op jit(solution)/shard_map/all_to_all | solution.py:58
  293.5 29.0 %all-to-all-start.6 = ((f32[1,192,3,192]{3,0,2,1:T(1,128)}), f32[1,192,3,192]{3,0,2,1:T(1,128)}, u32[]{:S(2)}, u32[]{:S(2)}) async-start(f32[1,192,3,192]{3,0,2,1:T(1,128)} %copy.284), calls=%async_computation.6 | async-start | bytes 1179648 | tf_op jit(solution)/shard_map/all_to_all | solution.py:57
  301.5 110.9 %all-reduce.2.cloned.1.call-start = ((), (), s32[]{:S(2)}) async-start(), calls=%async_computation.12 | async-start | bytes 1179648 | tf_op jit(solution)/shard_map/psum | solution.py:105
  330.8 1.5 copy-start.7
  412.4 3.9 copy-start.4
  422.1 34.3 %all-to-all-start.9 = ((f32[1,3,192,192]{3,0,1,2:T(1,128)}), f32[1,3,192,192]{3,0,1,2:T(1,128)}, u32[]{:S(2)}, u32[]{:S(2)}) async-start(f32[1,3,192,192]{3,0,1,2:T(1,128)} %copy.302), calls=%async_computation.9 | async-start | bytes 1179648 | tf_op jit(solution)/shard_map/all_to_all | solution.py:49
  456.3 29.2 %all-to-all-start.8 = ((f32[1,3,192,192]{3,0,1,2:T(1,128)}), f32[1,3,192,192]{3,0,1,2:T(1,128)S(1)}, u32[]{:S(2)}, u32[]{:S(2)}) async-start(f32[1,3,192,192]{3,0,1,2:T(1,128)} %copy.296), calls=%async_computation.8 | async-start | bytes 1179648 | tf_op jit(solution)/shard_map/all_to_all | solution.py:48
  486.7 1.4 copy-start.10
  489.5 1.5 copy-start.11
  496.8 29.1 %all-to-all-start.10 = ((f32[1,192,3,192]{3,0,2,1:T(1,128)}), f32[1,192,3,192]{3,0,2,1:T(1,128)}, u32[]{:S(2)}, u32[]{:S(2)}) async-start(f32[1,192,3,192]{3,0,2,1:T(1,128)} %copy.310), calls=%async_computation.10 | async-start | bytes 1179648 | tf_op jit(solution)/shard_map/all_to_all | solution.py:57
  507.6 26.0 %copy-start.12 = (f32[3,192,192]{2,1,0:T(8,128)S(1)}, f32[3,192,192]{2,1,0:T(8,128)}, u32[]{:S(2)}) copy-start(f32[3,192,192]{2,1,0:T(8,128)} %get-tuple-element.3) | copy-start | bytes 1327108
  526.0 28.9 %all-to-all-start.11 = ((f32[1,192,3,192]{3,0,2,1:T(1,128)}), f32[1,192,3,192]{3,0,2,1:T(1,128)S(1)}, u32[]{:S(2)}, u32[]{:S(2)}) async-start(f32[1,192,3,192]{3,0,2,1:T(1,128)} %copy.315), calls=%async_computation.11 | async-start | bytes 1179648 | tf_op jit(solution)/shard_map/all_to_all | solution.py:58
  554.9 0.8 copy-start.9
Sparse Core Ops, SparseCore 0:
  341.2 71.1 all-reduce.1
where the time goes:
time: 585 us; the launch traced here: 574 us
  waiting for transfers between devices  277 us (47%)
  matrix products  114 us (19%)
  starting transfers between devices  114 us (19%)
  local copies, waits for them, and re-layouts  52.3 us (9%)
  between operations  16 us (3%)
    psum x1, waiting for transfers between devices, local(): density = lax.psum(partial_value, 'band')  69.9 us
    all_to_all x3, waiting for transfers between devices, forward(): lax.all_to_all(real_part, 'grid', split_axis=2, concat_axis=1, tiled=True)  55.5 us
    all_to_all x3, waiting for transfers between devices, backward(): lax.all_to_all(imag_part, 'grid', split_axis=1, concat_axis=2, tiled=True)  53.6 us
    all_to_all x3, waiting for transfers between devices, backward(): lax.all_to_all(real_part, 'grid', split_axis=1, concat_axis=2, tiled=True)  50.5 us
    all_to_all x3, waiting for transfers between devices, forward(): lax.all_to_all(imag_part, 'grid', split_axis=2, concat_axis=1, tiled=True)  47.1 us
    all_to_all x3, starting transfers between devices, forward(): lax.all_to_all(imag_part, 'grid', split_axis=2, concat_axis=1, tiled=True)  41.4 us
    dot_general x18, matrix products, transform(): rc = jnp.einsum(form, real_part, cosine, precision=high)  30.9 us
    dot_general x17, matrix products, transform(): rs = jnp.einsum(form, real_part, sine, precision=high)  28.4 us
  transfers between devices with their start and end apart: 13, of which 13 were waited for; matrix products, arithmetic and copies ran while one was open for 8% of the time, Pallas kernels for 0%

commit v1 on v0

--- a/solution.py
+++ b/solution.py
@@ -55,7 +55,12 @@
     real_part, imag_part = along_x(real_part, imag_part, True)
     real_part, imag_part = (
         lax.all_to_all(real_part, "grid", split_axis=1, concat_axis=2, tiled=True),
-        lax.all_to_all(imag_part, "grid", split_axis=1, concat_axis=2, tiled=True),
+        jnp.concatenate(
+            lax.all_to_all(
+                jnp.stack(jnp.split(imag_part, lax.axis_size("grid"), axis=1)), "grid", 0, 0
+            ),
+            axis=2,
+        ),
     )
     real_part, imag_part = along_y(real_part, imag_part, True)
     real_part, imag_part = along_z(real_part, imag_part, True)

time: 585 us -> 579 us (0.990)
  waiting for transfers between devices: 277 us -> 265 us
    all_to_all x3, waiting for transfers between devices: 55.5 us -> 49.4 us  [forward(): lax.all_to_all(real_part, 'grid', split_axis=2, concat_axis=1, tiled=True)]
    another operation x12 -> x18, local copies, waits for them, and re-layouts: 12 us -> 16.3 us
  transfers between devices with their start and end apart: 13 -> 13, of which waited for: 13 -> 13; matrix products, arithmetic and copies ran while one was open for 8% -> 10% of each run, Pallas kernels for 0% -> 0%
where the time goes in v1:
time: 579 us; the launch traced here: 568 us
  waiting for transfers between devices  265 us (46%)
  matrix products  117 us (20%)
  starting transfers between devices  114 us (20%)
  local copies, waits for them, and re-layouts  54.4 us (9%)
  between operations  16.9 us (3%)
    psum x1, waiting for transfers between devices, local(): density = lax.psum(partial_value, 'band')  70.2 us
    all_to_all x3, waiting for transfers between devices, backward(): lax.all_to_all(real_part, 'grid', split_axis=1, concat_axis=2, tiled=True)  50 us
    all_to_all x3, waiting for transfers between devices, forward(): lax.all_to_all(real_part, 'grid', split_axis=2, concat_axis=1, tiled=True)  49.4 us
    all_to_all x3, waiting for transfers between devices, backward(): lax.all_to_all(jnp.stack(jnp.split(imag_part, lax.axis_size('grid'), axis...  49.3 us
    all_to_all x3, waiting for transfers between devices, forward(): lax.all_to_all(imag_part, 'grid', split_axis=2, concat_axis=1, tiled=True)  45.8 us
    all_to_all x3, starting transfers between devices, forward(): lax.all_to_all(imag_part, 'grid', split_axis=2, concat_axis=1, tiled=True)  41.2 us
    dot_general x17, matrix products, transform(): rs = jnp.einsum(form, real_part, sine, precision=high)  30.4 us
    dot_general x18, matrix products, transform(): rc = jnp.einsum(form, real_part, cosine, precision=high)  29.8 us
  transfers between devices with their start and end apart: 13, of which 13 were waited for; matrix products, arithmetic and copies ran while one was open for 10% of the time, Pallas kernels for 0%

profile of v1, /device:TPU:6, one launch (start us, length us, event | category | flops | bytes accessed | tf_op | source)
XLA Modules:
  0.0 568.4 jit_solution(5535399090222595006)
XLA Ops:
  7.2 3.1 fusion.60
  10.3 2.0 fusion.63
  12.3 2.0 fusion.55
  14.3 2.0 fusion.170
  16.3 2.0 fusion.54
  18.2 2.0 fusion.53
  22.1 19.1 %all-to-all-start = ((f32[1,3,192,192]{3,0,1,2:T(1,128)}), f32[1,3,192,192]{3,0,1,2:T(1,128)S(1)}, u32[]{:S(2)}, u32[]{:S(2)}) async-start(f32[1,3,192,192]{3,0,1,2:T(1,128)} %copy.331), calls=%async_computation | async-start | bytes 1179648 | tf_op jit(solution)/shard_map/all_to_all | solution.py:49
  41.3 2.0 fusion.166
  43.2 2.0 fusion.52
  46.6 14.3 %all-to-all-done = f32[1,3,192,192]{3,0,1,2:T(1,128)S(1)} async-done(((f32[1,3,192,192]{3,0,1,2:T(1,128)}), f32[1,3,192,192]{3,0,1,2:T(1,128)S(1)}, u32[]{:S(2)}, u32[]{:S(2)}) %all-to-all-start) | async-done | bytes 442400 | tf_op jit(solution)/shard_map/all_to_all | solution.py:49
  60.9 9.7 %all-to-all-start.1 = ((f32[1,3,192,192]{3,0,1,2:T(1,128)}), f32[1,3,192,192]{3,0,1,2:T(1,128)}, u32[]{:S(2)}, u32[]{:S(2)}) async-start(f32[1,3,192,192]{3,0,1,2:T(1,128)} %copy.339), calls=%async_computation.1 | async-start | bytes 1179648 | tf_op jit(solution)/shard_map/all_to_all | solution.py:48
  73.3 18.4 %all-to-all-done.1 = f32[1,3,192,192]{3,0,1,2:T(1,128)} async-done(((f32[1,3,192,192]{3,0,1,2:T(1,128)}), f32[1,3,192,192]{3,0,1,2:T(1,128)}, u32[]{:S(2)}, u32[]{:S(2)}) %all-to-all-start.1) | async-done | bytes 442400 | tf_op jit(solution)/shard_map/all_to_all | solution.py:48
  105.9 7.7 %all-to-all-start.2 = ((f32[64,1,3,3,192]{4,1,3,2,0:T(1,128)}), f32[64,1,3,3,192]{4,1,3,2,0:T(1,128)S(1)}, u32[]{:S(2)}, u32[]{:S(2)}) async-start(f32[64,1,3,3,192]{4,1,3,2,0:T(1,128)} %copy.347), calls=%async_computation.2 | async-start | bytes 1179648 | tf_op jit(solution)/shard_map/all_to_all | solution.py:59
  117.9 16.6 %all-to-all-done.2 = f32[64,1,3,3,192]{4,1,3,2,0:T(1,128)S(1)} async-done(((f32[64,1,3,3,192]{4,1,3,2,0:T(1,128)}), f32[64,1,3,3,192]{4,1,3,2,0:T(1,128)S(1)}, u32[]{:S(2)}, u32[]{:S(2)}) %all-to-all-start.2) | async-done | bytes 442400 | tf_op jit(solution)/shard_map/all_to_all | solution.py:59
  134.5 8.2 %all-to-all-start.3 = ((f32[1,192,3,192]{3,0,2,1:T(1,128)}), f32[1,192,3,192]{3,0,2,1:T(1,128)}, u32[]{:S(2)}, u32[]{:S(2)}) async-start(f32[1,192,3,192]{3,0,2,1:T(1,128)} %copy.352), calls=%async_computation.3 | async-start | bytes 1179648 | tf_op jit(solution)/shard_map/all_to_all | solution.py:57
  145.8 17.5 %all-to-all-done.3 = f32[1,192,3,192]{3,0,2,1:T(1,128)} async-done(((f32[1,192,3,192]{3,0,2,1:T(1,128)}), f32[1,192,3,192]{3,0,2,1:T(1,128)}, u32[]{:S(2)}, u32[]{:S(2)}) %all-to-all-start.3) | async-done | bytes 442400 | tf_op jit(solution)/shard_map/all_to_all | solution.py:57
  163.3 2.1 copy.353
  187.7 8.1 %all-to-all-start.5 = ((f32[1,3,192,192]{3,0,1,2:T(1,128)}), f32[1,3,192,192]{3,0,1,2:T(1,128)}, u32[]{:S(2)}, u32[]{:S(2)}) async-start(f32[1,3,192,192]{3,0,1,2:T(1,128)} %copy.365), calls=%async_computation.5 | async-start | bytes 1179648 | tf_op jit(solution)/shard_map/all_to_all | solution.py:49
  195.8 2.5 fusion.135
  201.2 15.4 %all-to-all-done.5 = f32[1,3,192,192]{3,0,1,2:T(1,128)} async-done(((f32[1,3,192,192]{3,0,1,2:T(1,128)}), f32[1,3,192,192]{3,0,1,2:T(1,128)}, u32[]{:S(2)}, u32[]{:S(2)}) %all-to-all-start.5) | async-done | bytes 442400 | tf_op jit(solution)/shard_map/all_to_all | solution.py:49
  216.6 8.2 %all-to-all-start.4 = ((f32[1,3,192,192]{3,0,1,2:T(1,128)}), f32[1,3,192,192]{3,0,1,2:T(1,128)}, u32[]{:S(2)}, u32[]{:S(2)}) async-start(f32[1,3,192,192]{3,0,1,2:T(1,128)} %copy.359), calls=%async_computation.4 | async-start | bytes 1179648 | tf_op jit(solution)/shard_map/all_to_all | solution.py:48
  229.0 2.3 fusion.131
  231.3 14.3 %all-to-all-done.4 = f32[1,3,192,192]{3,0,1,2:T(1,128)} async-done(((f32[1,3,192,192]{3,0,1,2:T(1,128)}), f32[1,3,192,192]{3,0,1,2:T(1,128)}, u32[]{:S(2)}, u32[]{:S(2)}) %all-to-all-start.4) | async-done | bytes 442400 | tf_op jit(solution)/shard_map/all_to_all | solution.py:48
  252.0 2.6 fusion.34
  261.6 7.9 %all-to-all-start.7 = ((f32[64,1,3,3,192]{4,1,3,2,0:T(1,128)}), f32[64,1,3,3,192]{4,1,3,2,0:T(1,128)}, u32[]{:S(2)}, u32[]{:S(2)}) async-start(f32[64,1,3,3,192]{4,1,3,2,0:T(1,128)} %copy.378), calls=%async_computation.7 | async-start | bytes 1179648 | tf_op jit(solution)/shard_map/all_to_all | solution.py:59
  269.5 2.5 fusion.139
  274.9 15.7 %all-to-all-done.7 = f32[64,1,3,3,192]{4,1,3,2,0:T(1,128)} async-done(((f32[64,1,3,3,192]{4,1,3,2,0:T(1,128)}), f32[64,1,3,3,192]{4,1,3,2,0:T(1,128)}, u32[]{:S(2)}, u32[]{:S(2)}) %all-to-all-start.7) | async-done | bytes 442400 | tf_op jit(solution)/shard_map/all_to_all | solution.py:59
  290.5 8.0 %all-to-all-start.6 = ((f32[1,192,3,192]{3,0,2,1:T(1,128)}), f32[1,192,3,192]{3,0,2,1:T(1,128)}, u32[]{:S(2)}, u32[]{:S(2)}) async-start(f32[1,192,3,192]{3,0,2,1:T(1,128)} %copy.373), calls=%async_computation.6 | async-start | bytes 1179648 | tf_op jit(solution)/shard_map/all_to_all | solution.py:57
  299.2 2.1 copy.379
  302.8 2.3 fusion.127
  305.1 14.3 %all-to-all-done.6 = f32[1,192,3,192]{3,0,2,1:T(1,128)} async-done(((f32[1,192,3,192]{3,0,2,1:T(1,128)}), f32[1,192,3,192]{3,0,2,1:T(1,128)}, u32[]{:S(2)}, u32[]{:S(2)}) %all-to-all-start.6) | async-done | bytes 442400 | tf_op jit(solution)/shard_map/all_to_all | solution.py:57
  319.4 2.1 copy.374
  321.6 2.2 reshape.451
  323.8 2.6 fusion.141
  333.6 3.0 add_multiply_fusion.1
  338.1 70.2 %all-reduce.2.cloned.1.call-done = f32[3,192,192]{2,1,0:T(8,128)} async-done(((f32[3,192,192]{2,1,0:T(8,128)}), f32[3,192,192]{2,1,0:T(8,128)}) %all-reduce.2.cloned.1.call-update) | async-done | bytes 442384 | tf_op jit(solution)/shard_map/psum | solution.py:110
  408.2 2.5 convolution_subtract_fusion.5
  417.9 14.0 %all-to-all-start.9 = ((f32[1,3,192,192]{3,0,1,2:T(1,128)}), f32[1,3,192,192]{3,0,1,2:T(1,128)}, u32[]{:S(2)}, u32[]{:S(2)}) async-start(f32[1,3,192,192]{3,0,1,2:T(1,128)} %copy.391), calls=%async_computation.9 | async-start | bytes 1179648 | tf_op jit(solution)/shard_map/all_to_all | solution.py:49
  436.1 16.0 %all-to-all-done.9 = f32[1,3,192,192]{3,0,1,2:T(1,128)} async-done(((f32[1,3,192,192]{3,0,1,2:T(1,128)}), f32[1,3,192,192]{3,0,1,2:T(1,128)}, u32[]{:S(2)}, u32[]{:S(2)}) %all-to-all-start.9) | async-done | bytes 442400 | tf_op jit(solution)/shard_map/all_to_all | solution.py:49
  452.2 7.7 %all-to-all-start.8 = ((f32[1,3,192,192]{3,0,1,2:T(1,128)}), f32[1,3,192,192]{3,0,1,2:T(1,128)S(1)}, u32[]{:S(2)}, u32[]{:S(2)}) async-start(f32[1,3,192,192]{3,0,1,2:T(1,128)} %copy.385), calls=%async_computation.8 | async-start | bytes 1179648 | tf_op jit(solution)/shard_map/all_to_all | solution.py:48
  462.1 2.3 fusion.115
  464.4 16.8 %all-to-all-done.8 = f32[1,3,192,192]{3,0,1,2:T(1,128)S(1)} async-done(((f32[1,3,192,192]{3,0,1,2:T(1,128)}), f32[1,3,192,192]{3,0,1,2:T(1,128)S(1)}, u32[]{:S(2)}, u32[]{:S(2)}) %all-to-all-start.8) | async-done | bytes 442400 | tf_op jit(solution)/shard_map/all_to_all | solution.py:48
  483.8 2.6 fusion.10
  493.4 7.5 %all-to-all-start.11 = ((f32[64,1,3,3,192]{4,1,3,2,0:T(1,128)}), f32[64,1,3,3,192]{4,1,3,2,0:T(1,128)S(1)}, u32[]{:S(2)}, u32[]{:S(2)}) async-start(f32[64,1,3,3,192]{4,1,3,2,0:T(1,128)} %copy.404), calls=%async_computation.11 | async-start | bytes 1179648 | tf_op jit(solution)/shard_map/all_to_all | solution.py:59
  505.2 17.0 %all-to-all-done.11 = f32[64,1,3,3,192]{4,1,3,2,0:T(1,128)S(1)} async-done(((f32[64,1,3,3,192]{4,1,3,2,0:T(1,128)}), f32[64,1,3,3,192]{4,1,3,2,0:T(1,128)S(1)}, u32[]{:S(2)}, u32[]{:S(2)}) %all-to-all-start.11) | async-done | bytes 442400 | tf_op jit(solution)/shard_map/all_to_all | solution.py:59
  522.2 7.7 %all-to-all-start.10 = ((f32[1,192,3,192]{3,0,2,1:T(1,128)}), f32[1,192,3,192]{3,0,2,1:T(1,128)}, u32[]{:S(2)}, u32[]{:S(2)}) async-start(f32[1,192,3,192]{3,0,2,1:T(1,128)} %copy.399), calls=%async_computation.10 | async-start | bytes 1179648 | tf_op jit(solution)/shard_map/all_to_all | solution.py:57
  533.0 18.2 %all-to-all-done.10 = f32[1,192,3,192]{3,0,2,1:T(1,128)} async-done(((f32[1,192,3,192]{3,0,2,1:T(1,128)}), f32[1,192,3,192]{3,0,2,1:T(1,128)}, u32[]{:S(2)}, u32[]{:S(2)}) %all-to-all-start.10) | async-done | bytes 442400 | tf_op jit(solution)/shard_map/all_to_all | solution.py:57
  558.5 2.6 fusion.1
  (320 shorter events, 119.8 us)
Async XLA Ops:
  7.2 3.1 copy-start
  22.1 38.8 %all-to-all-start = ((f32[1,3,192,192]{3,0,1,2:T(1,128)}), f32[1,3,192,192]{3,0,1,2:T(1,128)S(1)}, u32[]{:S(2)}, u32[]{:S(2)}) async-start(f32[1,3,192,192]{3,0,1,2:T(1,128)} %copy.331), calls=%async_computation | async-start | bytes 1179648 | tf_op jit(solution)/shard_map/all_to_all | solution.py:49
  60.9 30.7 %all-to-all-start.1 = ((f32[1,3,192,192]{3,0,1,2:T(1,128)}), f32[1,3,192,192]{3,0,1,2:T(1,128)}, u32[]{:S(2)}, u32[]{:S(2)}) async-start(f32[1,3,192,192]{3,0,1,2:T(1,128)} %copy.339), calls=%async_computation.1 | async-start | bytes 1179648 | tf_op jit(solution)/shard_map/all_to_all | solution.py:48
  105.9 28.6 %all-to-all-start.2 = ((f32[64,1,3,3,192]{4,1,3,2,0:T(1,128)}), f32[64,1,3,3,192]{4,1,3,2,0:T(1,128)S(1)}, u32[]{:S(2)}, u32[]{:S(2)}) async-start(f32[64,1,3,3,192]{4,1,3,2,0:T(1,128)} %copy.347), calls=%async_computation.2 | async-start | bytes 1179648 | tf_op jit(solution)/shard_map/all_to_all | solution.py:59
  116.4 26.3 %copy-start.14 = (f32[3,192,192]{2,1,0:T(8,128)S(1)}, f32[3,192,192]{2,1,0:T(8,128)}, u32[]{:S(2)}) copy-start(f32[3,192,192]{2,1,0:T(8,128)} %param.6) | copy-start | bytes 1327108
  116.4 26.3 %copy-start.15 = (f32[3,192,192]{2,1,0:T(8,128)S(1)}, f32[3,192,192]{2,1,0:T(8,128)}, u32[]{:S(2)}) copy-start(f32[3,192,192]{2,1,0:T(8,128)} %param.7) | copy-start | bytes 1327108
  134.5 8.4 %copy-start.10 = (f32[64,1,3,3,192]{4,1,3,2,0:T(1,128)}, f32[64,1,3,3,192]{4,1,3,2,0:T(1,128)S(1)}, u32[]{:S(2)}) copy-start(f32[64,1,3,3,192]{4,1,3,2,0:T(1,128)S(1)} %all-to-all-done.2) | copy-start | bytes 1327108
  134.5 28.9 %all-to-all-start.3 = ((f32[1,192,3,192]{3,0,2,1:T(1,128)}), f32[1,192,3,192]{3,0,2,1:T(1,128)}, u32[]{:S(2)}, u32[]{:S(2)}) async-start(f32[1,192,3,192]{3,0,2,1:T(1,128)} %copy.352), calls=%async_computation.3 | async-start | bytes 1179648 | tf_op jit(solution)/shard_map/all_to_all | solution.py:57
  184.0 0.8 copy-start.2
  187.7 28.9 %all-to-all-start.5 = ((f32[1,3,192,192]{3,0,1,2:T(1,128)}), f32[1,3,192,192]{3,0,1,2:T(1,128)}, u32[]{:S(2)}, u32[]{:S(2)}) async-start(f32[1,3,192,192]{3,0,1,2:T(1,128)} %copy.365), calls=%async_computation.5 | async-start | bytes 1179648 | tf_op jit(solution)/shard_map/all_to_all | solution.py:49
  216.6 28.9 %all-to-all-start.4 = ((f32[1,3,192,192]{3,0,1,2:T(1,128)}), f32[1,3,192,192]{3,0,1,2:T(1,128)}, u32[]{:S(2)}, u32[]{:S(2)}) async-start(f32[1,3,192,192]{3,0,1,2:T(1,128)} %copy.359), calls=%async_computation.4 | async-start | bytes 1179648 | tf_op jit(solution)/shard_map/all_to_all | solution.py:48
  229.0 18.0 %copy-start.4 = (f32[192,3,192]{2,0,1:T(8,128)}, f32[192,3,192]{2,0,1:T(8,128)S(1)}, u32[]{:S(2)}) copy-start(f32[192,3,192]{2,0,1:T(8,128)S(1)} %reshape.450) | copy-start | bytes 1327108
  249.7 0.8 copy-start.6
  250.6 1.4 copy-start.8
  252.0 4.0 copy-start.5
  257.5 1.9 copy-start.1
  261.6 28.9 %all-to-all-start.7 = ((f32[64,1,3,3,192]{4,1,3,2,0:T(1,128)}), f32[64,1,3,3,192]{4,1,3,2,0:T(1,128)}, u32[]{:S(2)}, u32[]{:S(2)}) async-start(f32[64,1,3,3,192]{4,1,3,2,0:T(1,128)} %copy.378), calls=%async_computation.7 | async-start | bytes 1179648 | tf_op jit(solution)/shard_map/all_to_all | solution.py:59
  290.5 28.9 %all-to-all-start.6 = ((f32[1,192,3,192]{3,0,2,1:T(1,128)}), f32[1,192,3,192]{3,0,2,1:T(1,128)}, u32[]{:S(2)}, u32[]{:S(2)}) async-start(f32[1,192,3,192]{3,0,2,1:T(1,128)} %copy.373), calls=%async_computation.6 | async-start | bytes 1179648 | tf_op jit(solution)/shard_map/all_to_all | solution.py:57
  298.5 109.7 %all-reduce.2.cloned.1.call-start = ((), (), s32[]{:S(2)}) async-start(), calls=%async_computation.12 | async-start | bytes 1179648 | tf_op jit(solution)/shard_map/psum | solution.py:110
  323.8 2.6 copy-start.7
  323.8 2.6 copy-start.9
  408.2 4.0 copy-start.3
  417.9 34.3 %all-to-all-start.9 = ((f32[1,3,192,192]{3,0,1,2:T(1,128)}), f32[1,3,192,192]{3,0,1,2:T(1,128)}, u32[]{:S(2)}, u32[]{:S(2)}) async-start(f32[1,3,192,192]{3,0,1,2:T(1,128)} %copy.391), calls=%async_computation.9 | async-start | bytes 1179648 | tf_op jit(solution)/shard_map/all_to_all | solution.py:49
  452.2 29.0 %all-to-all-start.8 = ((f32[1,3,192,192]{3,0,1,2:T(1,128)}), f32[1,3,192,192]{3,0,1,2:T(1,128)S(1)}, u32[]{:S(2)}, u32[]{:S(2)}) async-start(f32[1,3,192,192]{3,0,1,2:T(1,128)} %copy.385), calls=%async_computation.8 | async-start | bytes 1179648 | tf_op jit(solution)/shard_map/all_to_all | solution.py:48
  462.1 19.5 %copy-start.11 = (f32[192,3,192]{2,0,1:T(8,128)}, f32[192,3,192]{2,0,1:T(8,128)S(1)}, u32[]{:S(2)}) copy-start(f32[192,3,192]{2,0,1:T(8,128)S(1)} %reshape.457) | copy-start | bytes 1327108
  483.7 4.0 copy-start.12
  493.4 28.8 %all-to-all-start.11 = ((f32[64,1,3,3,192]{4,1,3,2,0:T(1,128)}), f32[64,1,3,3,192]{4,1,3,2,0:T(1,128)S(1)}, u32[]{:S(2)}, u32[]{:S(2)}) async-start(f32[64,1,3,3,192]{4,1,3,2,0:T(1,128)} %copy.404), calls=%async_computation.11 | async-start | bytes 1179648 | tf_op jit(solution)/shard_map/all_to_all | solution.py:59
  503.7 26.2 %copy-start.13 = (f32[3,192,192]{2,1,0:T(8,128)S(1)}, f32[3,192,192]{2,1,0:T(8,128)}, u32[]{:S(2)}) copy-start(f32[3,192,192]{2,1,0:T(8,128)} %get-tuple-element.3) | copy-start | bytes 1327108
  522.2 29.1 %all-to-all-start.10 = ((f32[1,192,3,192]{3,0,2,1:T(1,128)}), f32[1,192,3,192]{3,0,2,1:T(1,128)}, u32[]{:S(2)}, u32[]{:S(2)}) async-start(f32[1,192,3,192]{3,0,2,1:T(1,128)} %copy.399), calls=%async_computation.10 | async-start | bytes 1179648 | tf_op jit(solution)/shard_map/all_to_all | solution.py:57
Sparse Core Ops, SparseCore 0:
  336.8 71.3 all-reduce.1
